TPU v7x, 32 devices: a whole 2x2x4 slice. The times are simulated.
32 devices in a mesh: row: 4 (over z), col: 4 (over x, core), rhs: 2 (over y).
Axes of the slice: x: 2, y: 2, z: 4, core: 2. Of those that a mesh axis runs over, the one named last changes fastest.
Arguments:
- lower: float32 [6, 2048, 4, 2048], P(None, 'row', None, 'col'), may hold values from -0.0625 to 0.0625
- inverse: float32 [4, 2048, 2048], P(None, ('col', 'rhs'), 'row'), may hold values from -0.125 to 0.125
- right_side: float32 [6, 2048, 2048], P(None, 'row', 'rhs'), may hold values from -6 to 6
Outputs:
- solved: float32 [4, 2048, 2048], P(None, 'col', 'rhs')
- trailing: float32 [2, 2048, 2048], P(None, 'row', 'rhs')
All inputs are finite; a program needn't handle non-finite values.
Results may differ from a plain program's by a relative error of at most 0.0001.
Values sent between devices are 32-bit elements; how exact they have to be, the bound alone decides.
A program may use at most 128 MiB of HBM per device.

v0:
```python
import jax
import jax.numpy as jnp
from jax import lax
from jax.sharding import PartitionSpec as P


def apply_block(lower, unknowns, k):
    return jnp.einsum(
        "inc,cr->inr", lower[k + 1 :, :, k, :], unknowns, precision=lax.Precision.HIGHEST
    )


def solve_block(inverse, residual_block, k):
    inverse_rows = lax.all_gather(inverse[k], "rhs", axis=0, tiled=True)
    partial_value = jnp.dot(
        inverse_rows,
        residual_block,
        precision=lax.Precision.HIGHEST,
        preferred_element_type=jnp.float32,
    )
    return lax.psum(partial_value, "row")


def on_device(lower, inverse, right_side):
    chain_len = inverse.shape[0]
    solved_list = []
    partials = jnp.zeros_like(right_side)
    for k in range(chain_len):
        if k == 0:
            residual_block = right_side[0]
        else:
            residual_block = right_side[k] - lax.psum(partials[k], "col")
        unknowns = solve_block(inverse, residual_block, k)
        solved_list.append(unknowns)
        partials = jnp.concatenate(
            [partials[: k + 1], partials[k + 1 :] + apply_block(lower, unknowns, k)], axis=0
        )
    trailing = right_side[chain_len:] - lax.psum(partials[chain_len:], "col")
    return (jnp.stack(solved_list), trailing)


def solution(mesh):
    placed = (P(None, "row", None, "col"), P(None, ("col", "rhs"), "row"), P(None, "row", "rhs"))
    return jax.shard_map(
        on_device,
        mesh=mesh,
        in_specs=placed,
        out_specs=(P(None, "col", "rhs"), P(None, "row", "rhs")),
        check_vma=False,
    )
```

profile of v0, /device:TPU:0, one launch (start us, length us, event | category | flops | bytes accessed | tf_op | source)
XLA Modules:
  0.0 787.9 jit_solution(12352277579729281691)
XLA Ops:
  7.2 2.9 fusion.22
  10.1 0.0 all-reduce.9.cloned.1.call-start
  10.1 24.1 %all-gather.9.cloned.1.call-done = f32[1,512,512]{2,1,0:T(8,128)} async-done(((f32[1,256,512]{2,1,0:T(8,128)}), f32[1,512,512]{2,1,0:T(8,128)}) %all-gather.9.cloned.1.call-update) | async-done | bytes 1048592 | tf_op jit(solution)/shard_map/all_gather | solution.py:14
  34.3 6.8 fusion.11
  41.1 0.0 all-gather.11.cloned.1.call-start
  41.1 0.7 all-gather.11.cloned.1.call-update
  41.9 10.5 %slice.60 = f32[5,512,1,512]{3,2,1,0:T(1,128)} slice(f32[6,512,4,512]{3,2,1,0:T(4,128)} %param.3), slice={[1:6], [0:512], [0:1], [0:512]} | slice | bytes 10485760 | tf_op jit(solution)/shard_map/slice | solution.py:9
  52.3 75.4 %all-reduce.9.cloned.1.call-done = f32[512,1024]{1,0:T(8,128)} async-done(((f32[512,1024]{1,0:T(8,128)}), f32[512,1024]{1,0:T(8,128)}) %all-reduce.9.cloned.1.call-update) | async-done | bytes 2097168 | tf_op jit(solution)/shard_map/psum | solution.py:21
  127.7 40.3 %fusion.2 = f32[5,512,1024]{1,2,0:T(8,128)S(1)} fusion(f32[5,512,1,512]{3,2,1,0:T(1,128)} %slice.60, f32[512,1024]{1,0:T(8,128)} %all-reduce.9.cloned.1.call-done), kind=kOutput, calls=%fused_computation.8 | convolution fusion | flops 16106127360 | bytes 17825792 | tf_op jit(solution)/shard_map/inc,cr->inr/dot_general | solution.py:8
  168.1 4.0 copy-done
  172.1 1.5 slice_bitcast_fusion.2
  173.6 0.0 all-reduce.13.cloned.1.call-start
  173.6 5.8 fusion.21
  179.4 1.9 copy.32
  181.4 42.7 %all-reduce.11.cloned.1.call-done = f32[512,1024]{0,1:T(8,128)} async-done(((f32[512,1024]{0,1:T(8,128)}), f32[512,1024]{0,1:T(8,128)}) %all-reduce.11.cloned.1.call-update) | async-done | bytes 2097168 | tf_op jit(solution)/shard_map/psum | solution.py:32
  224.0 6.7 fusion.14
  230.8 0.0 all-gather.13.cloned.1.call-start
  230.8 0.5 all-gather.13.cloned.1.call-update
  231.4 9.0 %slice.65 = f32[4,512,1,512]{3,2,1,0:T(1,128)} slice(f32[6,512,4,512]{3,2,1,0:T(4,128)} %param.3), slice={[2:6], [0:512], [1:2], [0:512]} | slice | bytes 8388608 | tf_op jit(solution)/shard_map/slice | solution.py:9
  240.4 77.1 %all-reduce.13.cloned.1.call-done = f32[512,1024]{1,0:T(8,128)} async-done(((f32[512,1024]{1,0:T(8,128)}), f32[512,1024]{1,0:T(8,128)}) %all-reduce.13.cloned.1.call-update) | async-done | bytes 2097168 | tf_op jit(solution)/shard_map/psum | solution.py:21
  317.5 29.6 %slice_add_fusion = f32[4,512,1024]{1,2,0:T(8,128)S(1)} fusion(f32[5,512,1024]{1,2,0:T(8,128)} %copy-done, f32[4,512,1,512]{3,2,1,0:T(1,128)} %slice.65, f32[512,1024]{1,0:T(8,128)} %all-reduce.13.cloned.1.call-done), kind=kOutput, calls=%fused_computation | convolution fusion | flops 12886999040 | bytes 23068672 | tf_op jit(solution)/shard_map/inc,cr->inr/dot_general | solution.py:8
  347.1 3.4 copy-done.1
  350.5 1.5 slice_bitcast_fusion.1
  352.0 0.0 all-reduce.17.cloned.1.call-start
  352.1 2.1 copy.34
  354.2 48.3 %all-reduce.15.cloned.1.call-done = f32[512,1024]{0,1:T(8,128)} async-done(((f32[512,1024]{0,1:T(8,128)}), f32[512,1024]{0,1:T(8,128)}) %all-reduce.15.cloned.1.call-update) | async-done | bytes 2097168 | tf_op jit(solution)/shard_map/psum | solution.py:32
  402.5 6.7 fusion.15
  409.2 0.0 all-gather.15.cloned.1.call-start
  409.3 0.7 all-gather.15.cloned.1.call-update
  410.0 7.8 slice.70
  417.8 78.1 %all-reduce.17.cloned.1.call-done = f32[512,1024]{1,0:T(8,128)} async-done(((f32[512,1024]{1,0:T(8,128)}), f32[512,1024]{1,0:T(8,128)}) %all-reduce.17.cloned.1.call-update) | async-done | bytes 2097168 | tf_op jit(solution)/shard_map/psum | solution.py:21
  496.0 22.9 %slice_add_fusion.1 = f32[3,512,1024]{1,2,0:T(8,128)S(1)} fusion(f32[4,512,1024]{1,2,0:T(8,128)} %copy-done.1, f32[3,512,1,512]{3,2,1,0:T(1,128)S(1)} %slice.70, f32[512,1024]{1,0:T(8,128)} %all-reduce.17.cloned.1.call-done), kind=kOutput, calls=%fused_computation.2 | convolution fusion | flops 9665249280 | bytes 17825792 | tf_op jit(solution)/shard_map/inc,cr->inr/dot_general | solution.py:8
  518.9 2.7 copy-done.2
  521.6 1.5 slice_bitcast_fusion
  523.1 0.0 all-reduce.21.cloned.1.call-start
  523.2 2.2 copy.36
  525.4 48.2 %all-reduce.19.cloned.1.call-done = f32[512,1024]{0,1:T(8,128)} async-done(((f32[512,1024]{0,1:T(8,128)}), f32[512,1024]{0,1:T(8,128)}) %all-reduce.19.cloned.1.call-update) | async-done | bytes 2097168 | tf_op jit(solution)/shard_map/psum | solution.py:32
  573.6 6.7 fusion.16
  580.3 0.0 all-reduce.23.cloned.1.call-start
  580.4 5.5 slice.75
  585.9 81.2 %all-reduce.21.cloned.1.call-done = f32[512,1024]{1,0:T(8,128)} async-done(((f32[512,1024]{1,0:T(8,128)}), f32[512,1024]{1,0:T(8,128)}) %all-reduce.21.cloned.1.call-update) | async-done | bytes 2097168 | tf_op jit(solution)/shard_map/psum | solution.py:21
  667.1 17.1 %slice_add_fusion.2 = f32[2,512,1024]{1,2,0:T(8,128)} fusion(f32[3,512,1024]{1,2,0:T(8,128)} %copy-done.2, f32[2,512,1,512]{3,2,1,0:T(1,128)S(1)} %slice.75, f32[512,1024]{1,0:T(8,128)} %all-reduce.21.cloned.1.call-done), kind=kOutput, calls=%fused_computation.5 | convolution fusion | flops 6443499520 | bytes 12582912 | tf_op jit(solution)/shard_map/inc,cr->inr/dot_general | solution.py:8
  684.2 4.9 slice.73
  689.1 5.6 copy.38
  694.7 5.8 pad_maximum_fusion
  700.5 68.3 %all-reduce.23.cloned.1.call-done = f32[2,512,1024]{1,2,0:T(8,128)} async-done(((f32[2,512,1024]{1,2,0:T(8,128)}), f32[2,512,1024]{1,2,0:T(8,128)}) %all-reduce.23.cloned.1.call-update) | async-done | bytes 4194320 | tf_op jit(solution)/shard_map/psum | solution.py:38
  768.8 6.4 sub.15
  775.3 5.3 copy.20
  (21 shorter events, 0.4 us)
Async XLA Ops:
  7.2 27.1 %all-gather.9.cloned.1.call-start = ((), (), s32[]{:S(2)}) async-start(), calls=%async_computation.8 | async-start | bytes 1572864 | tf_op jit(solution)/shard_map/all_gather | solution.py:14
  10.1 117.6 %all-reduce.9.cloned.1.call-start = ((), (), s32[]{:S(2)}) async-start(), calls=%async_computation | async-start | bytes 4194304 | tf_op jit(solution)/shard_map/psum | solution.py:21
  41.1 140.3 %all-gather.11.cloned.1.call-start = ((), (), s32[]{:S(2)}) async-start(), calls=%async_computation.9 | async-start | bytes 1572864 | tf_op jit(solution)/shard_map/all_gather | solution.py:14
  41.8 182.2 %all-reduce.11.cloned.1.call-start = ((), (), s32[]{:S(2)}) async-start(), calls=%async_computation.1 | async-start | bytes 4194304 | tf_op jit(solution)/shard_map/psum | solution.py:32
  168.0 4.0 copy-start
  173.6 144.0 %all-reduce.13.cloned.1.call-start = ((), (), s32[]{:S(2)}) async-start(), calls=%async_computation.2 | async-start | bytes 4194304 | tf_op jit(solution)/shard_map/psum | solution.py:21
  230.8 123.4 %all-gather.13.cloned.1.call-start = ((), (), s32[]{:S(2)}) async-start(), calls=%async_computation.10 | async-start | bytes 1572864 | tf_op jit(solution)/shard_map/all_gather | solution.py:14
  231.3 171.2 %all-reduce.15.cloned.1.call-start = ((), (), s32[]{:S(2)}) async-start(), calls=%async_computation.3 | async-start | bytes 4194304 | tf_op jit(solution)/shard_map/psum | solution.py:32
  347.1 3.4 copy-start.1
  352.0 144.0 %all-reduce.17.cloned.1.call-start = ((), (), s32[]{:S(2)}) async-start(), calls=%async_computation.4 | async-start | bytes 4194304 | tf_op jit(solution)/shard_map/psum | solution.py:21
  409.2 116.1 %all-gather.15.cloned.1.call-start = ((), (), s32[]{:S(2)}) async-start(), calls=%async_computation.11 | async-start | bytes 1572864 | tf_op jit(solution)/shard_map/all_gather | solution.py:14
  410.0 163.6 %all-reduce.19.cloned.1.call-start = ((), (), s32[]{:S(2)}) async-start(), calls=%async_computation.5 | async-start | bytes 4194304 | tf_op jit(solution)/shard_map/psum | solution.py:32
  518.9 2.7 copy-start.2
  523.1 144.0 %all-reduce.21.cloned.1.call-start = ((), (), s32[]{:S(2)}) async-start(), calls=%async_computation.6 | async-start | bytes 4194304 | tf_op jit(solution)/shard_map/psum | solution.py:21
  580.3 188.5 %all-reduce.23.cloned.1.call-start = ((), (), s32[]{:S(2)}) async-start(), calls=%async_computation.7 | async-start | bytes 8388608 | tf_op jit(solution)/shard_map/psum | solution.py:38
  689.1 5.6 copy-start.3
Sparse Core Ops, SparseCore 0:
  10.2 23.9 all-gather.8
  41.2 86.4 all-reduce.8
  129.4 20.2 all-gather.10
  173.7 50.3 all-reduce.10
  230.9 86.5 all-reduce.12
  319.0 20.2 all-gather.12
  352.2 50.3 all-reduce.14
  409.4 86.5 all-reduce.16
  497.6 20.2 all-gather.14
  523.2 50.3 all-reduce.18
  580.4 86.5 all-reduce.20
  684.3 84.4 all-reduce.22
where the time goes:
time: 792 us; the launch traced here: 788 us
  waiting for transfers between devices  546 us (69%)
  matrix products  137 us (17%)
  local copies, waits for them, and re-layouts  78 us (10%)
  between operations  14.8 us (2%)
  other arithmetic  12.3 us (2%)
    psum x4, waiting for transfers between devices, solve_block(): return lax.psum(partial_value, 'row')  312 us
    psum x3, waiting for transfers between devices, on_device(): residual_block = right_side[k] - lax.psum(partials[k], 'col')  139 us
    dot_general x4, matrix products, apply_block(): jnp.einsum('inc,cr->inr', lower[k + 1:, :, k, :], unknowns, precision=lax...  110 us
    psum x1, waiting for transfers between devices, on_device(): trailing = right_side[chain_len:] - lax.psum(partials[chain_len:], 'col')  68.3 us
    slice x4, local copies, waits for them, and re-layouts, apply_block(): lower[k + 1:, :, k, :]  32.8 us
    unnamed x13, local copies, waits for them, and re-layouts  27.2 us
    dot_general x4, matrix products, solve_block(): jnp.dot(inverse_rows, residual_block, precision=lax.Precision.HIGHEST, pr...  26.9 us
    all_gather x4, waiting for transfers between devices, solve_block(): inverse_rows = lax.all_gather(inverse[k], 'rhs', axis=0, tiled=True)  24.2 us
  transfers between devices with their start and end apart: 12, of which 9 were waited for; matrix products, arithmetic and copies ran while one was open for 20% of the time, Pallas kernels for 0%

commit v1 on v0

v1 whole, which is shorter than its diff:
```python
import functools

import jax
import jax.numpy as jnp
from jax import lax
from jax.experimental import pallas as pl
from jax.experimental.pallas import tpu as pltpu
from jax.sharding import PartitionSpec as P

MESH = pl.DeviceIdType.MESH
LANES = 128


def split(value):
    high = value.astype(jnp.bfloat16)
    return high, (value - high.astype(jnp.float32)).astype(jnp.bfloat16)


def line_role(place, count):
    half = count // 2
    left = place < half
    inward = jnp.where(left, place + 1, place - 1)
    outward = jnp.where(left, place - 1, place + 1)
    from_end = jnp.where(left, place, count - 1 - place)
    return inward, outward, from_end, half - 1 - from_end


def kernel(
    dims, lower, inverse, right, solved, trailing,
    low_hi, low_lo, inv_hi, inv_lo, stage, inv_land, first, acc, zval, zin, zmid, x1, x2, x3, xin, pair,
    stage_sem, first_sem, acc_sem, inv_own_sem, inv_send, inv_recv,
    zin_recv, zmid_recv, z_in_send, z_out_send, sol_sem,
    x1_send, x1_recv, xin_recv, x2_recv, x_in_send, x_out_send, x3_send, x3_recv, tra_sem,
):
    rows_n, cols_n, rhs_n, chain, blocks, chunks, width = dims
    line_n = cols_n // 2
    zhalf, xhalf = rows_n // 2, line_n // 2
    mr, mc = acc.shape[2], zval.shape[1]
    mrh, mch = mr // 2, mc // 2
    lane_tiles = mc // LANES
    ways = lane_tiles * chain
    solved_at = rows_n - 1
    x_at = solved_at + 2
    last_at = x_at + line_n
    spacing = max(chunks, last_at + 1)
    slots = (chain - 1) * spacing + chunks + last_at

    me_row, me_col, me_rhs = lax.axis_index("row"), lax.axis_index("col"), lax.axis_index("rhs")
    core, chip = lax.rem(me_col, 2), lax.div(me_col, 2)
    sibling = me_col + 1 - 2 * core
    z_in, z_out, z_end, z_mid = line_role(me_row, rows_n)
    xc_in, xc_out, x_end, x_mid = line_role(chip, line_n)
    x_in, x_out = xc_in * 2 + core, xc_out * 2 + core
    own = pl.ds(pl.multiple_of(core * mrh, mrh), mrh)
    other = pl.ds(pl.multiple_of((1 - core) * mrh, mrh), mrh)

    barrier = pltpu.get_barrier_semaphore()

    def greet(device):
        pl.semaphore_signal(barrier, inc=1, device_id=device, device_id_type=MESH)

    greet({"row": z_in})
    greet({"col": sibling})
    greet({"col": x_in})
    for step in range(1, rhs_n):
        greet({"rhs": lax.rem(me_rhs + step, rhs_n)})
    if zhalf > 1:
        @pl.when(z_end > 0)
        def _():
            greet({"row": z_out})
    if xhalf > 1:
        @pl.when(x_end > 0)
        def _():
            greet({"col": x_out})
    count = 2 + rhs_n
    if zhalf > 1:
        count += (z_end > 0).astype(jnp.int32)
    if xhalf > 1:
        count += (x_end > 0).astype(jnp.int32)
    pl.semaphore_wait(barrier, count)

    def remote(src, dst, send, recv, device):
        return pltpu.make_async_remote_copy(
            src_ref=src, dst_ref=dst, send_sem=send, recv_sem=recv, device_id=device, device_id_type=MESH
        )

    part = inverse.shape[1]
    mine = pl.ds(pl.multiple_of(me_rhs * part, part), part)

    def inv_copy(k, step):
        return remote(
            inverse.at[k], inv_land.at[k, mine], inv_send.at[k, step - 1], inv_recv.at[k, step - 1],
            {"rhs": lax.rem(me_rhs + step, rhs_n)},
        )

    def inv_own(k):
        return pltpu.make_async_copy(inverse.at[k], inv_land.at[k, mine], inv_own_sem.at[k])

    for k in range(chain):
        for step in range(1, rhs_n):
            inv_copy(k, step).start()
        inv_own(k).start()

    def columns(c):
        return pl.ds(pl.multiple_of(c * width, width), width)

    def first_copy(c):
        return pltpu.make_async_copy(right.at[0, :, columns(c)], first.at[c], first_sem.at[c])

    def acc_copy(j, c):
        return pltpu.make_async_copy(right.at[j + 1, :, columns(c)], acc.at[j, c], acc_sem.at[j, c])

    def each_acc(action):
        @pl.loop(0, (blocks - 1) * chunks)
        def _(n):
            action(lax.div(n, chunks), lax.rem(n, chunks))

    @pl.loop(0, chunks)
    def _(c):
        first_copy(c).start()

    def stage_copy(n):
        i, half = 1 + lax.div(n, 2), lax.rem(n, 2)
        rows = pl.ds(pl.multiple_of(half * (mrh * ways), mrh * ways), mrh * ways)
        return pltpu.make_async_copy(lower.at[i, rows, :], stage.at[half], stage_sem.at[half])

    stage_copy(0).start()
    stage_copy(1).start()

    @pl.when(me_col == 0)
    def _():
        each_acc(lambda j, c: acc_copy(j, c).start())

    @pl.when(me_col != 0)
    def _():
        def clear(j, c):
            acc[j, c] = jnp.zeros((mr, width), jnp.float32)

        each_acc(clear)

    def place(k, i):
        return k * (blocks - 1) - lax.div(k * (k - 1), 2) + i - k - 1

    @pl.loop(0, 2 * (blocks - 1))
    def _(n):
        i, half = 1 + lax.div(n, 2), lax.rem(n, 2)
        rows = pl.ds(pl.multiple_of(half * mrh, mrh), mrh)
        stage_copy(n).wait()
        for k in range(chain):
            @pl.when(i > k)
            def _():
                spot = k * (blocks - 1) - (k * (k - 1)) // 2 + i - k - 1
                for tile in range(lane_tiles):
                    high, low = split(stage[half, pl.ds(tile * chain + k, mrh, stride=ways), :])
                    low_hi[spot, rows, pl.ds(tile * LANES, LANES)] = high
                    low_lo[spot, rows, pl.ds(tile * LANES, LANES)] = low

        @pl.when(n + 2 < 2 * (blocks - 1))
        def _():
            stage_copy(n + 2).start()

    @pl.loop(0, chunks)
    def _(c):
        first_copy(c).wait()

    @pl.when(me_col == 0)
    def _():
        each_acc(lambda j, c: acc_copy(j, c).wait())

    def product(high, low, depth):
        both = jnp.dot(high, pair[:depth, :], preferred_element_type=jnp.float32)
        rest = jnp.dot(low, pair[:depth, :width], preferred_element_type=jnp.float32)
        return both[:, :width] + (both[:, width:] + rest)

    def set_pair(rows, value):
        high, low = split(value)
        pair[rows, :width] = high
        pair[rows, width:] = low

    def z_rows(h):
        return pl.ds(h * mch, mch)

    def z_to_middle(k, c, h):
        return remote(zval.at[c, z_rows(h)], zmid.at[lax.rem(k, 2), c, z_rows(h)], z_in_send.at[c, h],
                      zmid_recv.at[lax.rem(k, 2), c, h], {"row": z_in})

    def z_inward(c, h):
        return remote(zval.at[c, z_rows(h)], zin.at[c, z_rows(h)], z_in_send.at[c, h], zin_recv.at[c, h], {"row": z_in})

    def z_outward(k, c, h):
        at = zmid.at[lax.rem(k, 2), c, z_rows(h)]
        return remote(at, at, z_out_send.at[c, h], zmid_recv.at[lax.rem(k, 2), c, h], {"row": z_out})

    def tail(j):
        return jnp.maximum(j - (chain - 1), 0)

    def x_first(j, c):
        return remote(acc.at[j, c, other], x1.at[tail(j), c], x1_send.at[j, c], x1_recv.at[j, c], {"col": sibling})

    def x_to_middle(j, c):
        return remote(acc.at[j, c, own], x2.at[j, c], x_in_send.at[j, c], x2_recv.at[j, c], {"col": x_in})

    def x_inward(j, c):
        return remote(acc.at[j, c, own], xin.at[j, c], x_in_send.at[j, c], xin_recv.at[j, c], {"col": x_in})

    def x_outward(j, c):
        return remote(x2.at[j, c], x2.at[j, c], x_out_send.at[j, c], x2_recv.at[j, c], {"col": x_out})

    def x_back(j, c):
        return remote(x2.at[j, c], x3.at[tail(j), c], x3_send.at[j, c], x3_recv.at[j, c], {"col": sibling})

    def solved_copy(k, c):
        return pltpu.make_async_copy(zmid.at[lax.rem(k, 2), c], solved.at[k, :, columns(c)], sol_sem.at[c])

    def trailing_own(j, c):
        return pltpu.make_async_copy(
            x2.at[j, c], trailing.at[j - (chain - 1), own, columns(c)], tra_sem.at[0, j - (chain - 1), c])

    def trailing_other(j, c):
        return pltpu.make_async_copy(
            x3.at[tail(j), c], trailing.at[j - (chain - 1), other, columns(c)], tra_sem.at[1, j - (chain - 1), c])

    def item(t, lag, then):
        u = t - lag
        n = jnp.maximum(u, 0)
        k, c = lax.div(n, spacing), lax.rem(n, spacing)

        @pl.when((u >= 0) & (k < chain) & (c < chunks))
        def _():
            then(k, c)

    def each_sum(k, action):
        stop = jnp.where(k == chain - 1, blocks - 1, k + 1)

        @pl.loop(k, stop)
        def _(j):
            action(j)

    def z_part(t, h):
        def inward_part(k, c):
            if zhalf > 1:
                @pl.when(z_end > 0)
                def _():
                    z_inward(c, h).wait_recv()
                    zval[c, z_rows(h)] += zin[c, z_rows(h)]

                @pl.when(z_mid > 0)
                def _():
                    z_inward(c, h).start()

            @pl.when(z_mid == 0)
            def _():
                z_to_middle(k, c, h).start()

        def outward_part(k, c):
            z_to_middle(k, c, h).wait_recv()

            @pl.when(z_mid == 0)
            def _():
                zmid[lax.rem(k, 2), c, z_rows(h)] += zval[c, z_rows(h)]

            if zhalf > 1:
                @pl.when(z_end > 0)
                def _():
                    z_outward(k, c, h).start()

        item(t, z_end, inward_part)
        item(t, zhalf + z_mid, outward_part)

    def x_part(t):
        def inward_part(k, c):
            def one(j):
                x_first(j, c).wait_recv()
                acc[j, c, own] += x1[tail(j), c]
                if xhalf > 1:
                    @pl.when(x_end > 0)
                    def _():
                        x_inward(j, c).wait_recv()
                        acc[j, c, own] += xin[j, c]

                    @pl.when(x_mid > 0)
                    def _():
                        x_inward(j, c).start()

                @pl.when(x_mid == 0)
                def _():
                    x_to_middle(j, c).start()

            each_sum(k, one)

        def outward_part(k, c):
            def one(j):
                x_to_middle(j, c).wait_recv()

                @pl.when(x_mid == 0)
                def _():
                    x2[j, c] += acc[j, c, own]

                x_back(j, c).start()
                if xhalf > 1:
                    @pl.when(x_end > 0)
                    def _():
                        x_outward(j, c).start()

            each_sum(k, one)

        def last_part(k, c):
            def one(j):
                x_back(j, c).wait_recv()
                x_first(j, c).wait_send()
                x_to_middle(j, c).wait_send()
                x_back(j, c).wait_send()
                if xhalf > 1:
                    @pl.when(x_end > 0)
                    def _():
                        x_outward(j, c).wait_send()

                @pl.when(k == chain - 1)
                def _():
                    trailing_own(j, c).start()
                    trailing_other(j, c).start()

            each_sum(k, one)

        item(t, x_at + x_end, inward_part)
        item(t, x_at + xhalf + x_mid, outward_part)
        item(t, last_at, last_part)

    def value_part(k, c):
        @pl.when(c == 0)
        def _():
            for step in range(1, rhs_n):
                inv_copy(k, step).wait()
            inv_own(k).wait()
            inv_hi[k], inv_lo[k] = split(inv_land[k])

        @pl.when(k == 0)
        def _():
            set_pair(pl.ds(0, mr), first[c])

        @pl.when(k > 0)
        def _():
            before = jnp.maximum(k - 1, 0)
            set_pair(own, x2[before, c])
            set_pair(other, x3[0, c])

        zval[c] = product(inv_hi[k], inv_lo[k], mr)

    def update_part(k, c):
        solved_copy(k, c).start()
        for h in range(2):
            z_inward(c, h).wait_send()
        set_pair(pl.ds(0, mc), zmid[lax.rem(k, 2), c])

        @pl.loop(k + 1, blocks)
        def _(i):
            spot = place(k, i)
            acc[i - 1, c] -= product(low_hi[spot], low_lo[spot], mc)

            @pl.when((i == k + 1) | (k == chain - 1))
            def _():
                x_first(i - 1, c).start()

    def release_part(k, c):
        solved_copy(k, c).wait()
        if zhalf > 1:
            @pl.when(z_end > 0)
            def _():
                for h in range(2):
                    z_outward(k, c, h).wait_send()

    @pl.loop(0, slots + 1)
    def _(n):
        t = n - 1
        z_part(t, 0)
        x_part(t)
        item(t, -1, value_part)
        z_part(t, 1)
        item(t, solved_at + 1, release_part)
        item(t, solved_at, update_part)

    @pl.loop(0, (blocks - chain) * chunks)
    def _(n):
        j, c = chain - 1 + lax.div(n, chunks), lax.rem(n, chunks)
        trailing_own(j, c).wait()
        trailing_other(j, c).wait()


def on_device(mesh, lower, inverse, right):
    rows_n, cols_n, rhs_n = mesh.shape["row"], mesh.shape["col"], mesh.shape["rhs"]
    blocks, mr, chain, mc = lower.shape
    width = LANES
    chunks = right.shape[2] // width
    part = inverse.shape[1]
    lane_tiles = mc // LANES
    flat = lower.reshape(blocks, mr, chain, lane_tiles, LANES).transpose(0, 1, 3, 2, 4)
    flat = flat.reshape(blocks, mr * lane_tiles * chain, LANES)
    pairs = sum(blocks - 1 - k for k in range(chain))
    sums = blocks - 1
    tails = blocks - chain
    mrh = mr // 2
    f32, bf16 = jnp.float32, jnp.bfloat16
    far = sums if cols_n > 4 else 1
    far_chunks = chunks if cols_n > 4 else 1
    dma = pltpu.SemaphoreType.DMA
    scratch = [
        pltpu.VMEM((pairs, mr, mc), bf16),
        pltpu.VMEM((pairs, mr, mc), bf16),
        pltpu.VMEM((chain, mc, mr), bf16),
        pltpu.VMEM((chain, mc, mr), bf16),
        pltpu.VMEM((2, mrh * lane_tiles * chain, LANES), f32),
        pltpu.VMEM((chain, mc, mr), f32),
        pltpu.VMEM((chunks, mr, width), f32),
        pltpu.VMEM((sums, chunks, mr, width), f32),
        pltpu.VMEM((chunks, mc, width), f32),
        pltpu.VMEM((chunks, mc, width), f32),
        pltpu.VMEM((2, chunks, mc, width), f32),
        pltpu.VMEM((tails, chunks, mrh, width), f32),
        pltpu.VMEM((sums, chunks, mrh, width), f32),
        pltpu.VMEM((tails, chunks, mrh, width), f32),
        pltpu.VMEM((far, far_chunks, mrh, width), f32),
        pltpu.VMEM((max(mr, mc), 2 * width), bf16),
        dma((2,)),
        dma((chunks,)),
        dma((sums, chunks)),
        dma((chain,)),
        dma((chain, rhs_n - 1)),
        dma((chain, rhs_n - 1)),
        dma((chunks, 2)),
        dma((2, chunks, 2)),
        dma((chunks, 2)),
        dma((chunks, 2)),
        dma((chunks,)),
        dma((sums, chunks)),
        dma((sums, chunks)),
        dma((far, far_chunks)),
        dma((sums, chunks)),
        dma((sums, chunks)),
        dma((sums, chunks)),
        dma((sums, chunks)),
        dma((sums, chunks)),
        dma((2, tails, chunks)),
    ]
    dims = (rows_n, cols_n, rhs_n, chain, blocks, chunks, width)
    any_spec = pl.BlockSpec(memory_space=pl.ANY)
    return pl.pallas_call(
        functools.partial(kernel, dims),
        out_shape=(
            jax.ShapeDtypeStruct((chain, mc, right.shape[2]), f32),
            jax.ShapeDtypeStruct((tails, mr, right.shape[2]), f32),
        ),
        in_specs=[any_spec] * 3,
        out_specs=(any_spec, any_spec),
        scratch_shapes=scratch,
        compiler_params=pltpu.CompilerParams(
            collective_id=0, has_side_effects=True, vmem_limit_bytes=62 * 1024 * 1024
        ),
        cost_estimate=pl.CostEstimate(
            flops=6 * (pairs + chain) * mr * mc * right.shape[2], bytes_accessed=4 * lower.size * 2, transcendentals=0
        ),
    )(flat, inverse, right)


def solution(mesh):
    placed = (P(None, "row", None, "col"), P(None, ("col", "rhs"), "row"), P(None, "row", "rhs"))
    return jax.shard_map(
        functools.partial(on_device, mesh),
        mesh=mesh,
        in_specs=placed,
        out_specs=(P(None, "col", "rhs"), P(None, "row", "rhs")),
        check_vma=False,
    )
```

time: 792 us -> 244 us (0.31)
  waiting for transfers between devices: 546 us -> 0 us
  Pallas kernels: 0 us -> 233 us
  matrix products: 137 us -> 0 us
  local copies, waits for them, and re-layouts: 78 us -> 10.6 us
  between operations: 14.8 us -> 0.65 us
  other arithmetic: 12.3 us -> 0 us
    psum x8 -> x0, waiting for transfers between devices: 519 us -> none  [the longest x4 312 us: solve_block(): return lax.psum(partial_value, 'row')]
    pallas_call x0 -> x1, Pallas kernels: none -> 233 us  [on_device(): pl.pallas_call(functools.partial(kernel, dims), out_shape=(jax.ShapeDtype...]
    dot_general x8 -> x0, matrix products: 137 us -> none  [the longest x4 110 us: apply_block(): jnp.einsum('inc,cr->inr', lower[k + 1:, :, k, :], unknowns, precision=lax...]
    slice x7 -> x0, local copies, waits for them, and re-layouts: 46.4 us -> none  [the longest x4 32.8 us: apply_block(): lower[k + 1:, :, k, :]]
    all_gather x4 -> x0, waiting for transfers between devices: 24.2 us -> none  [solve_block(): inverse_rows = lax.all_gather(inverse[k], 'rhs', axis=0, tiled=True)]
    unnamed x13 -> x4, local copies, waits for them, and re-layouts: 27.2 us -> 10.6 us
  transfers between devices with their start and end apart: 12 -> 0, of which waited for: 9 -> 0; matrix products, arithmetic and copies ran while one was open for 20% -> 0% of each run, Pallas kernels for 0% -> 0%
where the time goes in v1:
time: 244 us
  Pallas kernels  233 us (95%)
  local copies, waits for them, and re-layouts  10.6 us (4%)
    pallas_call x1, Pallas kernels, on_device(): pl.pallas_call(functools.partial(kernel, dims), out_shape=(jax.ShapeDtype...  233 us
    unnamed x4, local copies, waits for them, and re-layouts  10.6 us

profile of v1, /device:TPU:0, one launch (start us, length us, event | category | flops | bytes accessed | tf_op | source)
XLA Modules:
  0.0 244.1 jit_solution(9177371753690116896)
XLA Ops:
  0.6 232.8 %shard_map.50 = (f32[4,512,1024]{2,1,0:T(8,128)}, f32[2,512,1024]{2,1,0:T(8,128)}) custom-call(f32[6,8192,128]{2,1,0:T(8,128)} %bitcast.5, f32[4,256,512]{2,1,0:T(8,128)} %inverse.1, f32[6,512,1024]{2,1,0:T(8,128)} %right.1), custom_call_target="tpu_custom_call" | custom-call | flops 28991029248 | bytes 50331648 | tf_op jit(solution)/shard_map/pallas_call | solution.py:446
  233.5 0.0 copy-start
  233.5 8.6 %copy.8 = f32[4,512,1024]{2,1,0:T(8,128)} copy(f32[4,512,1024]{2,1,0:T(8,128)} %get-tuple-element.4) | data formatting | bytes 16777216
  242.1 0.0 copy-done
  242.1 2.0 copy.9
Async XLA Ops:
  233.5 8.6 %copy-start = (f32[2,512,1024]{2,1,0:T(8,128)S(1)}, f32[2,512,1024]{2,1,0:T(8,128)}, u32[]{:S(2)}) copy-start(f32[2,512,1024]{2,1,0:T(8,128)} %get-tuple-element.5) | copy-start | bytes 12582916

commit v2 on v1

--- a/solution.py
+++ b/solution.py
@@ -96,10 +96,12 @@
     def inv_own(k):
         return pltpu.make_async_copy(inverse.at[k], inv_land.at[k, mine], inv_own_sem.at[k])
 
-    for k in range(chain):
+    def inv_start(k):
         for step in range(1, rhs_n):
             inv_copy(k, step).start()
         inv_own(k).start()
+
+    inv_start(0)
 
     def columns(c):
         return pl.ds(pl.multiple_of(c * width, width), width)
@@ -332,6 +334,11 @@
             for step in range(1, rhs_n):
                 inv_copy(k, step).wait()
             inv_own(k).wait()
+
+            @pl.when(k + 1 < chain)
+            def _():
+                inv_start(k + 1)
+
             inv_hi[k], inv_lo[k] = split(inv_land[k])
 
         @pl.when(k == 0)
@@ -384,6 +391,20 @@
         j, c = chain - 1 + lax.div(n, chunks), lax.rem(n, chunks)
         trailing_own(j, c).wait()
         trailing_other(j, c).wait()
+
+
+def hand_over(solved, trailing, solved_out, trailing_out, solved_sem, trailing_sem):
+    copies = []
+    for src, dst, sems in ((solved, solved_out, solved_sem), (trailing, trailing_out, trailing_sem)):
+        rows = src.shape[1] // 2
+        for k in range(src.shape[0]):
+            for half in range(2):
+                at = pl.ds(half * rows, rows)
+                copies.append(pltpu.make_async_copy(src.at[k, at], dst.at[k, at], sems.at[k, half]))
+    for copy in copies:
+        copy.start()
+    for copy in copies:
+        copy.wait()
 
 
 def on_device(mesh, lower, inverse, right):
@@ -443,7 +464,7 @@
     ]
     dims = (rows_n, cols_n, rhs_n, chain, blocks, chunks, width)
     any_spec = pl.BlockSpec(memory_space=pl.ANY)
-    return pl.pallas_call(
+    found = pl.pallas_call(
         functools.partial(kernel, dims),
         out_shape=(
             jax.ShapeDtypeStruct((chain, mc, right.shape[2]), f32),
@@ -459,6 +480,17 @@
             flops=6 * (pairs + chain) * mr * mc * right.shape[2], bytes_accessed=4 * lower.size * 2, transcendentals=0
         ),
     )(flat, inverse, right)
+    shapes = tuple(jax.ShapeDtypeStruct(array.shape, array.dtype) for array in found)
+    return pl.pallas_call(
+        hand_over,
+        out_shape=shapes,
+        in_specs=[any_spec] * 2,
+        out_specs=(any_spec, any_spec),
+        scratch_shapes=[dma((chain, 2)), dma((tails, 2))],
+        cost_estimate=pl.CostEstimate(
+            flops=0, bytes_accessed=8 * sum(array.size for array in found), transcendentals=0
+        ),
+    )(*found)
 
 
 def solution(mesh):

time: 244 us -> 616 us (2.52)
  Pallas kernels: 233 us -> 615 us
  local copies, waits for them, and re-layouts: 10.6 us -> 0 us
    pallas_call x0 -> x1, Pallas kernels: none -> 382 us  [on_device(): pl.pallas_call(hand_over, out_shape=shapes, in_specs=[any_spec] * 2, out_...]
    unnamed x4 -> x0, local copies, waits for them, and re-layouts: 10.6 us -> none
where the time goes in v2:
time: 616 us
  Pallas kernels  615 us (100%)
    pallas_call x1, Pallas kernels, on_device(): pl.pallas_call(hand_over, out_shape=shapes, in_specs=[any_spec] * 2, out_...  382 us
    pallas_call x1, Pallas kernels, on_device(): pl.pallas_call(functools.partial(kernel, dims), out_shape=(jax.ShapeDtype...  233 us

profile of v2, /device:TPU:0, one launch (start us, length us, event | category | flops | bytes accessed | tf_op | source)
XLA Modules:
  0.0 615.5 jit_solution(2730946732840421830)
XLA Ops:
  0.6 232.5 %shard_map.50 = (f32[4,512,1024]{2,1,0:T(8,128)}, f32[2,512,1024]{2,1,0:T(8,128)}) custom-call(f32[6,8192,128]{2,1,0:T(8,128)} %bitcast.5, f32[4,256,512]{2,1,0:T(8,128)} %inverse.1, f32[6,512,1024]{2,1,0:T(8,128)} %right.1), custom_call_target="tpu_custom_call" | custom-call | flops 28991029248 | bytes 50331648 | tf_op jit(solution)/shard_map/pallas_call | solution.py:467
  233.2 382.4 %shard_map.51 = (f32[4,512,1024]{2,1,0:T(8,128)}, f32[2,512,1024]{2,1,0:T(8,128)}) custom-call(f32[4,512,1024]{2,1,0:T(8,128)} %get-tuple-element.4.solved, f32[2,512,1024]{2,1,0:T(8,128)} %get-tuple-element.5.trailing), custom_call_target="tpu_custom_call" | custom-call | bytes 25165824 | tf_op jit(solution)/shard_map/pallas_call | solution.py:484

commit v3 on v2

--- a/solution.py
+++ b/solution.py
@@ -37,8 +37,6 @@
     zhalf, xhalf = rows_n // 2, line_n // 2
     mr, mc = acc.shape[2], zval.shape[1]
     mrh, mch = mr // 2, mc // 2
-    lane_tiles = mc // LANES
-    ways = lane_tiles * chain
     solved_at = rows_n - 1
     x_at = solved_at + 2
     last_at = x_at + line_n
@@ -121,13 +119,34 @@
     def _(c):
         first_copy(c).start()
 
-    def stage_copy(n):
-        i, half = 1 + lax.div(n, 2), lax.rem(n, 2)
-        rows = pl.ds(pl.multiple_of(half * (mrh * ways), mrh * ways), mrh * ways)
-        return pltpu.make_async_copy(lower.at[i, rows, :], stage.at[half], stage_sem.at[half])
-
-    stage_copy(0).start()
-    stage_copy(1).start()
+    pairs, slot_n = low_hi.shape[0], stage.shape[0]
+
+    def place(k, i):
+        return k * (blocks - 1) - lax.div(k * (k - 1), 2) + i - k - 1
+
+    def stage_copy(spot, action):
+        for k in range(chain):
+            begin = k * (blocks - 1) - (k * (k - 1)) // 2
+            end = begin + blocks - 1 - k
+
+            @pl.when((spot >= begin) & (spot < end))
+            def _():
+                at = lax.rem(spot, slot_n)
+                action(pltpu.make_async_copy(lower.at[spot - begin + k + 1, :, k, :], stage.at[at], stage_sem.at[at]))
+
+    def take_block(spot):
+        @pl.when((spot >= 0) & (spot < pairs))
+        def _():
+            stage_copy(spot, lambda copy: copy.wait())
+            low_hi[spot], low_lo[spot] = split(stage[lax.rem(spot, slot_n)])
+
+            @pl.when(spot + slot_n < pairs)
+            def _():
+                stage_copy(spot + slot_n, lambda copy: copy.start())
+
+    @pl.loop(0, min(slot_n, pairs))
+    def _(spot):
+        stage_copy(spot, lambda copy: copy.start())
 
     @pl.when(me_col == 0)
     def _():
@@ -140,34 +159,11 @@
 
         each_acc(clear)
 
-    def place(k, i):
-        return k * (blocks - 1) - lax.div(k * (k - 1), 2) + i - k - 1
-
-    @pl.loop(0, 2 * (blocks - 1))
-    def _(n):
-        i, half = 1 + lax.div(n, 2), lax.rem(n, 2)
-        rows = pl.ds(pl.multiple_of(half * mrh, mrh), mrh)
-        stage_copy(n).wait()
-        for k in range(chain):
-            @pl.when(i > k)
-            def _():
-                spot = k * (blocks - 1) - (k * (k - 1)) // 2 + i - k - 1
-                for tile in range(lane_tiles):
-                    high, low = split(stage[half, pl.ds(tile * chain + k, mrh, stride=ways), :])
-                    low_hi[spot, rows, pl.ds(tile * LANES, LANES)] = high
-                    low_lo[spot, rows, pl.ds(tile * LANES, LANES)] = low
-
-        @pl.when(n + 2 < 2 * (blocks - 1))
-        def _():
-            stage_copy(n + 2).start()
+    take_block(0)
 
     @pl.loop(0, chunks)
     def _(c):
         first_copy(c).wait()
-
-    @pl.when(me_col == 0)
-    def _():
-        each_acc(lambda j, c: acc_copy(j, c).wait())
 
     def product(high, low, depth):
         both = jnp.dot(high, pair[:depth, :], preferred_element_type=jnp.float32)
@@ -384,7 +380,13 @@
         item(t, -1, value_part)
         z_part(t, 1)
         item(t, solved_at + 1, release_part)
+
+        @pl.when((t == 0) & (me_col == 0))
+        def _():
+            each_acc(lambda j, c: acc_copy(j, c).wait())
+
         item(t, solved_at, update_part)
+        take_block(t + 2)
 
     @pl.loop(0, (blocks - chain) * chunks)
     def _(n):
@@ -393,18 +395,26 @@
         trailing_other(j, c).wait()
 
 
-def hand_over(solved, trailing, solved_out, trailing_out, solved_sem, trailing_sem):
-    copies = []
-    for src, dst, sems in ((solved, solved_out, solved_sem), (trailing, trailing_out, trailing_sem)):
+def hand_over(solved, trailing, solved_out, trailing_out, solved_buf, trailing_buf, solved_sem, trailing_sem):
+    jobs = []
+    for src, buf, dst, sems in (
+        (solved, solved_buf, solved_out, solved_sem), (trailing, trailing_buf, trailing_out, trailing_sem),
+    ):
         rows = src.shape[1] // 2
         for k in range(src.shape[0]):
             for half in range(2):
                 at = pl.ds(half * rows, rows)
-                copies.append(pltpu.make_async_copy(src.at[k, at], dst.at[k, at], sems.at[k, half]))
-    for copy in copies:
-        copy.start()
-    for copy in copies:
-        copy.wait()
+                jobs.append((
+                    pltpu.make_async_copy(src.at[k, at], buf.at[k, at], sems.at[0, k, half]),
+                    pltpu.make_async_copy(buf.at[k, at], dst.at[k, at], sems.at[1, k, half]),
+                ))
+    for come, _ in jobs:
+        come.start()
+    for come, go in jobs:
+        come.wait()
+        go.start()
+    for _, go in jobs:
+        go.wait()
 
 
 def on_device(mesh, lower, inverse, right):
@@ -413,11 +423,9 @@
     width = LANES
     chunks = right.shape[2] // width
     part = inverse.shape[1]
-    lane_tiles = mc // LANES
-    flat = lower.reshape(blocks, mr, chain, lane_tiles, LANES).transpose(0, 1, 3, 2, 4)
-    flat = flat.reshape(blocks, mr * lane_tiles * chain, LANES)
     pairs = sum(blocks - 1 - k for k in range(chain))
     sums = blocks - 1
+    stages = min(4, pairs)
     tails = blocks - chain
     mrh = mr // 2
     f32, bf16 = jnp.float32, jnp.bfloat16
@@ -429,7 +437,7 @@
         pltpu.VMEM((pairs, mr, mc), bf16),
         pltpu.VMEM((chain, mc, mr), bf16),
         pltpu.VMEM((chain, mc, mr), bf16),
-        pltpu.VMEM((2, mrh * lane_tiles * chain, LANES), f32),
+        pltpu.VMEM((stages, mr, mc), f32),
         pltpu.VMEM((chain, mc, mr), f32),
         pltpu.VMEM((chunks, mr, width), f32),
         pltpu.VMEM((sums, chunks, mr, width), f32),
@@ -441,7 +449,7 @@
         pltpu.VMEM((tails, chunks, mrh, width), f32),
         pltpu.VMEM((far, far_chunks, mrh, width), f32),
         pltpu.VMEM((max(mr, mc), 2 * width), bf16),
-        dma((2,)),
+        dma((stages,)),
         dma((chunks,)),
         dma((sums, chunks)),
         dma((chain,)),
@@ -479,14 +487,19 @@
         cost_estimate=pl.CostEstimate(
             flops=6 * (pairs + chain) * mr * mc * right.shape[2], bytes_accessed=4 * lower.size * 2, transcendentals=0
         ),
-    )(flat, inverse, right)
+    )(lower, inverse, right)
     shapes = tuple(jax.ShapeDtypeStruct(array.shape, array.dtype) for array in found)
     return pl.pallas_call(
         hand_over,
         out_shape=shapes,
         in_specs=[any_spec] * 2,
         out_specs=(any_spec, any_spec),
-        scratch_shapes=[dma((chain, 2)), dma((tails, 2))],
+        scratch_shapes=[
+            *(pltpu.VMEM(shape.shape, shape.dtype) for shape in shapes),
+            dma((2, chain, 2)),
+            dma((2, tails, 2)),
+        ],
+        compiler_params=pltpu.CompilerParams(vmem_limit_bytes=32 * 1024 * 1024),
         cost_estimate=pl.CostEstimate(
             flops=0, bytes_accessed=8 * sum(array.size for array in found), transcendentals=0
         ),

time: 616 us -> 243 us (0.39)
  Pallas kernels: 615 us -> 236 us
    pallas_call x1, Pallas kernels: 382 us -> 5.61 us  [on_device(): pl.pallas_call(hand_over, out_shape=shapes, in_specs=[any_spec] * 2, out_...]
where the time goes in v3:
time: 243 us; the launch traced here: 242 us
  Pallas kernels  236 us (97%)
  local copies, waits for them, and re-layouts  5.56 us (2%)
    pallas_call x1, Pallas kernels, on_device(): pl.pallas_call(functools.partial(kernel, dims), out_shape=(jax.ShapeDtype...  231 us
    pallas_call x1, Pallas kernels, on_device(): pl.pallas_call(hand_over, out_shape=shapes, in_specs=[any_spec] * 2, out_...  5.61 us
    unnamed x4, local copies, waits for them, and re-layouts  5.56 us

profile of v3, /device:TPU:0, one launch (start us, length us, event | category | flops | bytes accessed | tf_op | source)
XLA Modules:
  0.0 242.3 jit_solution(12368138466685434995)
XLA Ops:
  0.6 230.5 %shard_map.50 = (f32[4,512,1024]{2,1,0:T(8,128)}, f32[2,512,1024]{2,1,0:T(8,128)}) custom-call(f32[6,512,4,512]{3,2,1,0:T(4,128)} %lower.1, f32[4,256,512]{2,1,0:T(8,128)} %inverse.1, f32[6,512,1024]{2,1,0:T(8,128)} %right.1), custom_call_target="tpu_custom_call" | custom-call | flops 28991029248 | bytes 50331648 | tf_op jit(solution)/shard_map/pallas_call | solution.py:475
  231.1 0.0 copy-start
  231.2 3.4 %copy-done = f32[4,512,1024]{2,1,0:T(8,128)S(1)} copy-done((f32[4,512,1024]{2,1,0:T(8,128)S(1)}, f32[4,512,1024]{2,1,0:T(8,128)}, u32[]{:S(2)}) %copy-start) | copy-done | bytes 8388632
  234.5 0.0 copy-start.1
  234.5 2.2 copy-done.1
  236.7 5.6 %shard_map.51 = (f32[4,512,1024]{2,1,0:T(8,128)}, f32[2,512,1024]{2,1,0:T(8,128)}) custom-call(f32[4,512,1024]{2,1,0:T(8,128)S(1)} %copy-done, f32[2,512,1024]{2,1,0:T(8,128)S(1)} %copy-done.1), custom_call_target="tpu_custom_call" | custom-call | bytes 25165824 | tf_op jit(solution)/shard_map/pallas_call | solution.py:492
Async XLA Ops:
  231.1 3.4 %copy-start = (f32[4,512,1024]{2,1,0:T(8,128)S(1)}, f32[4,512,1024]{2,1,0:T(8,128)}, u32[]{:S(2)}) copy-start(f32[4,512,1024]{2,1,0:T(8,128)} %get-tuple-element.4.solved) | copy-start | bytes 25165828
  234.5 2.2 copy-start.1

commit v4 on v3

--- a/solution.py
+++ b/solution.py
@@ -27,7 +27,7 @@
 
 def kernel(
     dims, lower, inverse, right, solved, trailing,
-    low_hi, low_lo, inv_hi, inv_lo, stage, inv_land, first, acc, zval, zin, zmid, x1, x2, x3, xin, pair,
+    low_hi, low_lo, inv_hi, inv_lo, stage, inv_land, first, acc, zval, zin, zmid, x1, x2, x3, xin, pair, duo,
     stage_sem, first_sem, acc_sem, inv_own_sem, inv_send, inv_recv,
     zin_recv, zmid_recv, z_in_send, z_out_send, sol_sem,
     x1_send, x1_recv, xin_recv, x2_recv, x_in_send, x_out_send, x3_send, x3_recv, tra_sem,
@@ -38,7 +38,7 @@
     mr, mc = acc.shape[2], zval.shape[1]
     mrh, mch = mr // 2, mc // 2
     solved_at = rows_n - 1
-    x_at = solved_at + 2
+    x_at = solved_at + 1
     last_at = x_at + line_n
     spacing = max(chunks, last_at + 1)
     slots = (chain - 1) * spacing + chunks + last_at
@@ -355,14 +355,40 @@
             z_inward(c, h).wait_send()
         set_pair(pl.ds(0, mc), zmid[lax.rem(k, 2), c])
 
-        @pl.loop(k + 1, blocks)
+        @pl.loop(k + 1, jnp.where(k == chain - 1, blocks, k + 2))
         def _(i):
             spot = place(k, i)
             acc[i - 1, c] -= product(low_hi[spot], low_lo[spot], mc)
-
-            @pl.when((i == k + 1) | (k == chain - 1))
-            def _():
-                x_first(i - 1, c).start()
+            x_first(i - 1, c).start()
+
+        @pl.when(k < chain - 1)
+        def _():
+            for odd in range(2):
+                @pl.when(lax.rem(c, 2) == odd)
+                def _():
+                    duo[:, odd * width:(odd + 1) * width] = pair[:mc, :width]
+                    duo[:, (odd + 2) * width:(odd + 3) * width] = pair[:mc, width:]
+
+            @pl.when(lax.rem(c, 2) == 1)
+            def _():
+                update_two(k, c, k + 2, jnp.minimum(k + 4, blocks))
+
+    def update_two(k, c, begin, end):
+        before = jnp.maximum(c - 1, 0)
+
+        @pl.loop(begin, end)
+        def _(i):
+            spot = place(k, i)
+            wide = jnp.dot(low_hi[spot], duo[...], preferred_element_type=jnp.float32)
+            rest = jnp.dot(low_lo[spot], duo[:, :2 * width], preferred_element_type=jnp.float32)
+            both = wide[:, :2 * width] + (wide[:, 2 * width:] + rest)
+            acc[i - 1, before] -= both[:, :width]
+            acc[i - 1, c] -= both[:, width:]
+
+    def rest_part(k, c):
+        @pl.when((k < chain - 1) & (lax.rem(c, 2) == 1))
+        def _():
+            update_two(k, c, k + 4, jnp.maximum(blocks, k + 4))
 
     def release_part(k, c):
         solved_copy(k, c).wait()
@@ -385,6 +411,7 @@
         def _():
             each_acc(lambda j, c: acc_copy(j, c).wait())
 
+        item(t, solved_at + 1, rest_part)
         item(t, solved_at, update_part)
         take_block(t + 2)
 
@@ -422,6 +449,7 @@
     blocks, mr, chain, mc = lower.shape
     width = LANES
     chunks = right.shape[2] // width
+    assert chunks % 2 == 0
     part = inverse.shape[1]
     pairs = sum(blocks - 1 - k for k in range(chain))
     sums = blocks - 1
@@ -449,6 +477,7 @@
         pltpu.VMEM((tails, chunks, mrh, width), f32),
         pltpu.VMEM((far, far_chunks, mrh, width), f32),
         pltpu.VMEM((max(mr, mc), 2 * width), bf16),
+        pltpu.VMEM((mc, 4 * width), bf16),
         dma((stages,)),
         dma((chunks,)),
         dma((sums, chunks)),
@@ -499,7 +528,7 @@
             dma((2, chain, 2)),
             dma((2, tails, 2)),
         ],
-        compiler_params=pltpu.CompilerParams(vmem_limit_bytes=32 * 1024 * 1024),
+        compiler_params=pltpu.CompilerParams(vmem_limit_bytes=62 * 1024 * 1024),
         cost_estimate=pl.CostEstimate(
             flops=0, bytes_accessed=8 * sum(array.size for array in found), transcendentals=0
         ),

time: 243 us -> 237 us (0.975)
  local copies, waits for them, and re-layouts: 5.56 us -> 0 us
    unnamed x4 -> x0, local copies, waits for them, and re-layouts: 5.56 us -> none
    pallas_call x1, Pallas kernels: 5.61 us -> 9.17 us  [on_device(): pl.pallas_call(hand_over, out_shape=shapes, in_specs=[any_spec] * 2, out_...]
    pallas_call x1, Pallas kernels: 231 us -> 227 us  [on_device(): pl.pallas_call(functools.partial(kernel, dims), out_shape=(jax.ShapeDtype...]
where the time goes in v4:
time: 237 us
  Pallas kernels  237 us (100%)
    pallas_call x1, Pallas kernels, on_device(): pl.pallas_call(functools.partial(kernel, dims), out_shape=(jax.ShapeDtype...  227 us
    pallas_call x1, Pallas kernels, on_device(): pl.pallas_call(hand_over, out_shape=shapes, in_specs=[any_spec] * 2, out_...  9.17 us

profile of v4, /device:TPU:0, one launch (start us, length us, event | category | flops | bytes accessed | tf_op | source)
XLA Modules:
  0.0 237.2 jit_solution(5916946781017297946)
XLA Ops:
  0.6 227.4 %shard_map.50 = (f32[4,512,1024]{2,1,0:T(8,128)}, f32[2,512,1024]{2,1,0:T(8,128)}) custom-call(f32[6,512,4,512]{3,2,1,0:T(4,128)} %lower.1, f32[4,256,512]{2,1,0:T(8,128)} %inverse.1, f32[6,512,1024]{2,1,0:T(8,128)} %right.1), custom_call_target="tpu_custom_call" | custom-call | flops 28991029248 | bytes 50331648 | tf_op jit(solution)/shard_map/pallas_call | solution.py:504
  228.0 9.2 %shard_map.51 = (f32[4,512,1024]{2,1,0:T(8,128)}, f32[2,512,1024]{2,1,0:T(8,128)}) custom-call(f32[4,512,1024]{2,1,0:T(8,128)} %get-tuple-element.4.solved, f32[2,512,1024]{2,1,0:T(8,128)} %get-tuple-element.5.trailing), custom_call_target="tpu_custom_call" | custom-call | bytes 25165824 | tf_op jit(solution)/shard_map/pallas_call | solution.py:521

commit v5 on v4

--- a/solution.py
+++ b/solution.py
@@ -9,6 +9,7 @@
 
 MESH = pl.DeviceIdType.MESH
 LANES = 128
+PARTS = 4
 
 
 def split(value):
@@ -36,7 +37,7 @@
     line_n = cols_n // 2
     zhalf, xhalf = rows_n // 2, line_n // 2
     mr, mc = acc.shape[2], zval.shape[1]
-    mrh, mch = mr // 2, mc // 2
+    mrh, mch = mr // 2, mc // PARTS
     solved_at = rows_n - 1
     x_at = solved_at + 1
     last_at = x_at + line_n
@@ -351,7 +352,7 @@
 
     def update_part(k, c):
         solved_copy(k, c).start()
-        for h in range(2):
+        for h in range(PARTS):
             z_inward(c, h).wait_send()
         set_pair(pl.ds(0, mc), zmid[lax.rem(k, 2), c])
 
@@ -361,6 +362,7 @@
             acc[i - 1, c] -= product(low_hi[spot], low_lo[spot], mc)
             x_first(i - 1, c).start()
 
+    def far_part(k, c):
         @pl.when(k < chain - 1)
         def _():
             for odd in range(2):
@@ -395,24 +397,27 @@
         if zhalf > 1:
             @pl.when(z_end > 0)
             def _():
-                for h in range(2):
+                for h in range(PARTS):
                     z_outward(k, c, h).wait_send()
 
     @pl.loop(0, slots + 1)
     def _(n):
         t = n - 1
-        z_part(t, 0)
+        for h in range(PARTS // 2):
+            z_part(t, h)
         x_part(t)
         item(t, -1, value_part)
-        z_part(t, 1)
+        item(t, solved_at + 1, rest_part)
+        for h in range(PARTS // 2, PARTS):
+            z_part(t, h)
         item(t, solved_at + 1, release_part)
 
         @pl.when((t == 0) & (me_col == 0))
         def _():
             each_acc(lambda j, c: acc_copy(j, c).wait())
 
-        item(t, solved_at + 1, rest_part)
         item(t, solved_at, update_part)
+        item(t, solved_at, far_part)
         take_block(t + 2)
 
     @pl.loop(0, (blocks - chain) * chunks)
@@ -484,10 +489,10 @@
         dma((chain,)),
         dma((chain, rhs_n - 1)),
         dma((chain, rhs_n - 1)),
-        dma((chunks, 2)),
-        dma((2, chunks, 2)),
-        dma((chunks, 2)),
-        dma((chunks, 2)),
+        dma((chunks, PARTS)),
+        dma((2, chunks, PARTS)),
+        dma((chunks, PARTS)),
+        dma((chunks, PARTS)),
         dma((chunks,)),
         dma((sums, chunks)),
         dma((sums, chunks)),

time: 237 us -> 236 us (level)
  no operation moved by 1% of the time
where the time goes in v5:
time: 236 us
  Pallas kernels  235 us (100%)
    pallas_call x1, Pallas kernels, on_device(): pl.pallas_call(functools.partial(kernel, dims), out_shape=(jax.ShapeDtype...  226 us
    pallas_call x1, Pallas kernels, on_device(): pl.pallas_call(hand_over, out_shape=shapes, in_specs=[any_spec] * 2, out_...  9.17 us

profile of v5, /device:TPU:0, one launch (start us, length us, event | category | flops | bytes accessed | tf_op | source)
XLA Modules:
  0.0 236.1 jit_solution(118040639719602169)
XLA Ops:
  0.6 226.3 %shard_map.50 = (f32[4,512,1024]{2,1,0:T(8,128)}, f32[2,512,1024]{2,1,0:T(8,128)}) custom-call(f32[6,512,4,512]{3,2,1,0:T(4,128)} %lower.1, f32[4,256,512]{2,1,0:T(8,128)} %inverse.1, f32[6,512,1024]{2,1,0:T(8,128)} %right.1), custom_call_target="tpu_custom_call" | custom-call | flops 28991029248 | bytes 50331648 | tf_op jit(solution)/shard_map/pallas_call | solution.py:509
  226.9 9.2 %shard_map.51 = (f32[4,512,1024]{2,1,0:T(8,128)}, f32[2,512,1024]{2,1,0:T(8,128)}) custom-call(f32[4,512,1024]{2,1,0:T(8,128)} %get-tuple-element.4.solved, f32[2,512,1024]{2,1,0:T(8,128)} %get-tuple-element.5.trailing), custom_call_target="tpu_custom_call" | custom-call | bytes 25165824 | tf_op jit(solution)/shard_map/pallas_call | solution.py:526

commit v6 on v5

--- a/solution.py
+++ b/solution.py
@@ -10,6 +10,7 @@
 MESH = pl.DeviceIdType.MESH
 LANES = 128
 PARTS = 4
+EARLY = 2
 
 
 def split(value):
@@ -149,19 +150,6 @@
     def _(spot):
         stage_copy(spot, lambda copy: copy.start())
 
-    @pl.when(me_col == 0)
-    def _():
-        each_acc(lambda j, c: acc_copy(j, c).start())
-
-    @pl.when(me_col != 0)
-    def _():
-        def clear(j, c):
-            acc[j, c] = jnp.zeros((mr, width), jnp.float32)
-
-        each_acc(clear)
-
-    take_block(0)
-
     @pl.loop(0, chunks)
     def _(c):
         first_copy(c).wait()
@@ -176,8 +164,11 @@
         pair[rows, :width] = high
         pair[rows, width:] = low
 
+    own_parts = PARTS // rhs_n
+
     def z_rows(h):
-        return pl.ds(h * mch, mch)
+        at = lax.rem(h + me_rhs * own_parts, PARTS)
+        return pl.ds(pl.multiple_of(at * mch, mch), mch)
 
     def z_to_middle(k, c, h):
         return remote(zval.at[c, z_rows(h)], zmid.at[lax.rem(k, 2), c, z_rows(h)], z_in_send.at[c, h],
@@ -235,7 +226,7 @@
         def _(j):
             action(j)
 
-    def z_part(t, h):
+    def z_steps(h):
         def inward_part(k, c):
             if zhalf > 1:
                 @pl.when(z_end > 0)
@@ -263,8 +254,19 @@
                 def _():
                     z_outward(k, c, h).start()
 
-        item(t, z_end, inward_part)
-        item(t, zhalf + z_mid, outward_part)
+        return inward_part, outward_part
+
+    def z_part(t, h):
+        for lag, step in zip((z_end, zhalf + z_mid), z_steps(h)):
+            def once(k, c, step=step):
+                if h >= own_parts:
+                    step(k, c)
+                else:
+                    @pl.when((k > 0) | (c >= EARLY))
+                    def _():
+                        step(k, c)
+
+            item(t, lag, once)
 
     def x_part(t):
         def inward_part(k, c):
@@ -330,7 +332,10 @@
         def _():
             for step in range(1, rhs_n):
                 inv_copy(k, step).wait()
-            inv_own(k).wait()
+
+            @pl.when(k > 0)
+            def _():
+                inv_own(k).wait()
 
             @pl.when(k + 1 < chain)
             def _():
@@ -348,7 +353,18 @@
             set_pair(own, x2[before, c])
             set_pair(other, x3[0, c])
 
-        zval[c] = product(inv_hi[k], inv_lo[k], mr)
+        @pl.when((k > 0) | (c >= EARLY))
+        def _():
+            zval[c] = product(inv_hi[k], inv_lo[k], mr)
+
+        @pl.when((k == 0) & (c < EARLY))
+        def _():
+            for step in range(1, rhs_n):
+                value_rows(0, c, lax.rem(me_rhs + step, rhs_n))
+
+    def value_rows(k, c, group):
+        rows = pl.ds(pl.multiple_of(group * part, part), part)
+        zval[c, rows] = product(inv_hi[k, rows], inv_lo[k, rows], mr)
 
     def update_part(k, c):
         solved_copy(k, c).start()
@@ -399,6 +415,31 @@
             def _():
                 for h in range(PARTS):
                     z_outward(k, c, h).wait_send()
+
+    inv_own(0).wait()
+    inv_hi[0, mine], inv_lo[0, mine] = split(inv_land[0, mine])
+    for c in range(EARLY):
+        set_pair(pl.ds(0, mr), first[c])
+        value_rows(0, c, me_rhs)
+        for h in range(own_parts):
+            z_steps(h)[0](0, c)
+    @pl.when(me_col == 0)
+    def _():
+        each_acc(lambda j, c: acc_copy(j, c).start())
+
+    @pl.when(me_col != 0)
+    def _():
+        def clear(j, c):
+            acc[j, c] = jnp.zeros((mr, width), jnp.float32)
+
+        each_acc(clear)
+
+    taken = min(4, pairs)
+    for spot in range(taken):
+        take_block(spot)
+    for c in range(EARLY):
+        for h in range(own_parts):
+            z_steps(h)[1](0, c)
 
     @pl.loop(0, slots + 1)
     def _(n):
@@ -418,7 +459,7 @@
 
         item(t, solved_at, update_part)
         item(t, solved_at, far_part)
-        take_block(t + 2)
+        take_block(t + 1 + taken)
 
     @pl.loop(0, (blocks - chain) * chunks)
     def _(n):

time: 236 us -> 235 us (level)
  no operation moved by 1% of the time
where the time goes in v6:
time: 235 us
  Pallas kernels  234 us (100%)
    pallas_call x1, Pallas kernels, on_device(): pl.pallas_call(functools.partial(kernel, dims), out_shape=(jax.ShapeDtype...  225 us
    pallas_call x1, Pallas kernels, on_device(): pl.pallas_call(hand_over, out_shape=shapes, in_specs=[any_spec] * 2, out_...  9.17 us

profile of v6, /device:TPU:0, one launch (start us, length us, event | category | flops | bytes accessed | tf_op | source)
XLA Modules:
  0.0 235.0 jit_solution(5164769122525423530)
XLA Ops:
  0.6 225.2 %shard_map.50 = (f32[4,512,1024]{2,1,0:T(8,128)}, f32[2,512,1024]{2,1,0:T(8,128)}) custom-call(f32[6,512,4,512]{3,2,1,0:T(4,128)} %lower.1, f32[4,256,512]{2,1,0:T(8,128)} %inverse.1, f32[6,512,1024]{2,1,0:T(8,128)} %right.1), custom_call_target="tpu_custom_call" | custom-call | flops 28991029248 | bytes 50331648 | tf_op jit(solution)/shard_map/pallas_call | solution.py:550
  225.8 9.2 %shard_map.51 = (f32[4,512,1024]{2,1,0:T(8,128)}, f32[2,512,1024]{2,1,0:T(8,128)}) custom-call(f32[4,512,1024]{2,1,0:T(8,128)} %get-tuple-element.4.solved, f32[2,512,1024]{2,1,0:T(8,128)} %get-tuple-element.5.trailing), custom_call_target="tpu_custom_call" | custom-call | bytes 25165824 | tf_op jit(solution)/shard_map/pallas_call | solution.py:567

commit v7 on v6

--- a/solution.py
+++ b/solution.py
@@ -434,7 +434,7 @@
 
         each_acc(clear)
 
-    taken = min(4, pairs)
+    taken = min(2, pairs)
     for spot in range(taken):
         take_block(spot)
     for c in range(EARLY):
@@ -459,7 +459,7 @@
 
         item(t, solved_at, update_part)
         item(t, solved_at, far_part)
-        take_block(t + 1 + taken)
+        take_block(jnp.where(t + 1 >= taken, t + 1, -1))
 
     @pl.loop(0, (blocks - chain) * chunks)
     def _(n):

time: 235 us -> 235 us (level)
  no operation moved by 1% of the time
where the time goes in v7:
time: 235 us
  Pallas kernels  234 us (100%)
    pallas_call x1, Pallas kernels, on_device(): pl.pallas_call(functools.partial(kernel, dims), out_shape=(jax.ShapeDtype...  225 us
    pallas_call x1, Pallas kernels, on_device(): pl.pallas_call(hand_over, out_shape=shapes, in_specs=[any_spec] * 2, out_...  9.17 us

profile of v7, /device:TPU:0, one launch (start us, length us, event | category | flops | bytes accessed | tf_op | source)
XLA Modules:
  0.0 234.5 jit_solution(9915267220089464530)
XLA Ops:
  0.6 224.7 %shard_map.50 = (f32[4,512,1024]{2,1,0:T(8,128)}, f32[2,512,1024]{2,1,0:T(8,128)}) custom-call(f32[6,512,4,512]{3,2,1,0:T(4,128)} %lower.1, f32[4,256,512]{2,1,0:T(8,128)} %inverse.1, f32[6,512,1024]{2,1,0:T(8,128)} %right.1), custom_call_target="tpu_custom_call" | custom-call | flops 28991029248 | bytes 50331648 | tf_op jit(solution)/shard_map/pallas_call | solution.py:550
  225.3 9.2 %shard_map.51 = (f32[4,512,1024]{2,1,0:T(8,128)}, f32[2,512,1024]{2,1,0:T(8,128)}) custom-call(f32[4,512,1024]{2,1,0:T(8,128)} %get-tuple-element.4.solved, f32[2,512,1024]{2,1,0:T(8,128)} %get-tuple-element.5.trailing), custom_call_target="tpu_custom_call" | custom-call | bytes 25165824 | tf_op jit(solution)/shard_map/pallas_call | solution.py:567
